TPU v7x, 32 devices: a whole 2x2x4 slice. The times are simulated.
32 devices in a mesh: blk: 8 (over z, y), dp: 4 (over x, core).
Axes of the slice: x: 2, y: 2, z: 4, core: 2. Of those that a mesh axis runs over, the one named last changes fastest.
Arguments:
- tokens: bfloat16 [12288, 4096], P(('blk', 'dp')), may hold values from -6 to 6
- grad_k: bfloat16 [12288, 1024], P(('blk', 'dp')), may hold values from -6 to 6
- adapter_a: bfloat16 [4096, 192], P('blk'), may hold values from -0.09375 to 0.09375
- adapter_b: bfloat16 [192, 1024], P('blk'), may hold values from -0.1875 to 0.1875
Outputs:
- grad_a: float32 [4096, 192], P('blk')
- grad_b: float32 [192, 1024], P('blk')
All inputs are finite; a program needn't handle non-finite values.
Results may differ from a plain program's by a relative error of at most 0.003.
Values may be sent and summed in bfloat16 or wider, within the bound.
A program may use at most 64 MiB of HBM per device.

v0:
```python
import math

import jax
import jax.numpy as jnp
from jax import lax
from jax.sharding import PartitionSpec as P


def shards(tokens, grad_k, adapter_a, adapter_b):
    count = lax.axis_size("blk")
    rows_a = adapter_a.shape[0]
    rows_b = adapter_b.shape[0]
    rank = rows_b * count
    width_k = grad_k.shape[1]
    factor = 1.0 / math.sqrt(tokens.shape[0] * count * lax.axis_size("dp"))
    columns = tokens
    hidden = jnp.dot(
        columns,
        lax.all_gather(adapter_a, "blk", axis=0, tiled=True),
        preferred_element_type=jnp.float32,
    ).astype(jnp.bfloat16)
    spread = lax.dot_general(
        grad_k,
        lax.all_gather(adapter_b, "blk", axis=0, tiled=True),
        (((1,), (1,)), ((), ())),
        preferred_element_type=jnp.float32,
    ).astype(jnp.bfloat16)
    columns = tokens
    part_a = lax.dot_general(
        columns, spread, (((0,), (0,)), ((), ())), preferred_element_type=jnp.float32
    )
    part_b = lax.dot_general(
        hidden, grad_k, (((0,), (0,)), ((), ())), preferred_element_type=jnp.float32
    )
    joined = jnp.concatenate(
        [
            part_a.reshape(1 * lax.axis_size("blk"), rows_a * rank),
            part_b.reshape(1 * lax.axis_size("blk"), rows_b * width_k),
        ],
        axis=1,
    )
    share = lax.psum_scatter(joined * factor, "blk", scatter_dimension=0, tiled=True)
    owned_a = share[0, : rows_a * rank].reshape(rows_a, rank)
    owned_b = share[0, rows_a * rank :].reshape(rows_b, width_k)
    grad_a, grad_b = lax.psum((owned_a, owned_b), "dp")
    return (grad_a, grad_b)


def solution(mesh):
    return jax.shard_map(
        shards,
        mesh=mesh,
        in_specs=(P(("blk", "dp"), None), P(("blk", "dp"), None), P("blk", None), P("blk", None)),
        out_specs=(P("blk", None), P("blk", None)),
        check_vma=False,
    )
```

profile of v0, /device:TPU:1, one launch (start us, length us, event | category | flops | bytes accessed | tf_op | source)
XLA Modules:
  0.0 266.2 jit_solution(14328088110151087768)
XLA Ops:
  7.2 0.0 all-gather.2.cloned.1.call-start
  7.2 0.7 all-gather.2.cloned.1.call-update
  7.9 0.0 all-reduce.5.cloned.1.call-start
  8.0 27.2 %all_gather.6 = bf16[192,1024]{1,0:T(8,128)(2,1)S(1)} all-gather(bf16[24,1024]{1,0:T(8,128)(2,1)} %param.7), channel_id=1, replica_groups=mesh['blk'=8,'dp'=4] {'blk'}, dimensions={0}, use_global_device_ids=true | all-gather | bytes 442368 | tf_op jit(solution)/shard_map/all_gather | solution.py:24
  35.2 4.2 %convolution_bitcast_fusion = f32[4096,192]{0,1:T(8,128)} fusion(bf16[384,4096]{1,0:T(8,128)(2,1)S(1)} %copy-done, bf16[384,1024]{1,0:T(8,128)(2,1)} %param.5, bf16[192,1024]{1,0:T(8,128)(2,1)S(1)} %all_gather.6), kind=kOutput, calls=%fused_computation | convolution fusion | flops 755048448 | bytes 7471104 | tf_op jit(solution)/shard_map/dot_general | solution.py:29
  39.4 5.2 %copy.8 = f32[4096,192]{1,0:T(8,128)} copy(f32[4096,192]{0,1:T(8,128)} %convolution_bitcast_fusion) | data formatting | bytes 6291456 | tf_op jit(solution)/shard_map/dot_general | solution.py:29
  44.5 5.6 %reshape.10 = f32[8,98304]{1,0:T(8,128)} reshape(f32[4096,192]{1,0:T(8,128)} %copy.8) | data formatting | bytes 6291456 | tf_op jit(solution)/shard_map/reshape | solution.py:37
  50.2 7.2 %all-gather.2.cloned.1.call-done = bf16[4096,192]{0,1:T(8,128)(2,1)} async-done(((bf16[512,192]{0,1:T(8,128)(2,1)}), bf16[4096,192]{0,1:T(8,128)(2,1)}) %all-gather.2.cloned.1.call-update) | async-done | bytes 1572880 | tf_op jit(solution)/shard_map/all_gather | solution.py:19
  57.4 4.2 %fusion = f32[192,1024]{1,0:T(8,128)} fusion(bf16[384,1024]{1,0:T(8,128)(2,1)} %param.5, bf16[384,4096]{1,0:T(8,128)(2,1)S(1)} %copy-done, bf16[4096,192]{0,1:T(8,128)(2,1)} %all-gather.2.cloned.1.call-done), kind=kOutput, calls=%fused_computation.4 | convolution fusion | flops 755048448 | bytes 6291456 | tf_op jit(solution)/shard_map/dot_general | solution.py:32
  61.6 2.2 reshape.11
  63.8 4.3 %maximum_multiply_fusion = f32[8,122880]{1,0:T(8,128)} fusion(f32[8,24576]{1,0:T(8,128)} %reshape.11, f32[8,98304]{1,0:T(8,128)} %reshape.10), kind=kLoop, calls=%fused_computation.1 | loop fusion | flops 1966080 | bytes 7864320 | tf_op jit(solution)/shard_map/mul | solution.py:42
  68.1 0.0 all-reduce.5.cloned.1.call-update
  68.1 0.0 all-reduce.7.cloned.1.call-start
  68.2 0.6 copy-done.1
  68.8 0.6 dynamic-slice
  69.3 147.7 %all-reduce.5.cloned.1.call-done = f32[8,122880]{1,0:T(8,128)} async-done(((f32[8,122880]{1,0:T(8,128)}), f32[8,122880]{1,0:T(8,128)}) %all-reduce.5.cloned.1.call-update) | async-done | bytes 3932176
  217.0 3.6 %dynamic-slice_reduce_fusion = f32[98304]{0:T(1024)S(1)} fusion(f32[8,122880]{1,0:T(8,128)} %all-reduce.5.cloned.1.call-done, u32[]{:T(128)} %bitcast.1), kind=kLoop, calls=%fused_computation.5 | loop fusion | bytes 786436 | tf_op jit(solution)/shard_map/slice | solution.py:43
  220.6 0.9 reshape_squeeze.6
  221.5 2.1 dynamic-slice_reduce_fusion.1
  223.6 0.7 reshape_squeeze.7
  224.3 0.0 all-reduce.7.cloned.1.call-update
  224.3 31.9 %all-reduce.7.cloned.1.call-done = (f32[512,192]{1,0:T(8,128)}, f32[24,1024]{1,0:T(8,128)}) async-done(((f32[512,192]{1,0:T(8,128)}, f32[24,1024]{1,0:T(8,128)}), (f32[512,192]{1,0:T(8,128)}, f32[24,1024]{1,0:T(8,128)})) %all-reduce.7.cloned.1.call-update) | async-done | bytes 491536 | tf_op jit(solution)/shard_map/psum | solution.py:45
  256.2 2.0 copy.9
  258.2 1.5 copy.13
  (3 shorter events, 0.0 us)
Async XLA Ops:
  7.2 28.0 %copy-start = (bf16[384,4096]{1,0:T(8,128)(2,1)S(1)}, bf16[384,4096]{1,0:T(8,128)(2,1)}, u32[]{:S(2)}) copy-start(bf16[384,4096]{1,0:T(8,128)(2,1)} %param.4) | copy-start | bytes 9437188
  7.2 50.2 %all-gather.2.cloned.1.call-start = ((), (), s32[]{:S(2)}) async-start(), calls=%async_computation | async-start | bytes 1769472 | tf_op jit(solution)/shard_map/all_gather | solution.py:19
  7.9 209.1 %all-reduce.5.cloned.1.call-start = ((), (), s32[]{:S(2)}) async-start(), calls=%async_computation.1 | async-start | bytes 7864320
  68.1 0.7 copy-start.1
  68.1 188.1 %all-reduce.7.cloned.1.call-start = ((), (), s32[]{:S(2)}) async-start(), calls=%async_computation.2 | async-start | bytes 1245184 | tf_op jit(solution)/shard_map/psum | solution.py:45
Sparse Core Ops, SparseCore 0:
  10.1 47.2 all-gather.1
  68.2 148.7 all-reduce.4
  224.4 31.7 all-reduce.6
where the time goes:
time: 269 us; the launch traced here: 266 us
  waiting for transfers between devices  187 us (70%)
  blocking collectives  27.2 us (10%)
  local copies, waits for them, and re-layouts  24.9 us (9%)
  between operations  13.8 us (5%)
  matrix products  8.45 us (3%)
  other arithmetic  4.34 us (2%)
    unnamed x4, waiting for transfers between devices  148 us
    psum x1, waiting for transfers between devices, shards(): grad_a, grad_b = lax.psum((owned_a, owned_b), 'dp')  31.9 us
    all_gather x1, blocking collectives, shards(): lax.all_gather(adapter_b, 'blk', axis=0, tiled=True)  27.2 us
    all_gather x1, waiting for transfers between devices, shards(): lax.all_gather(adapter_a, 'blk', axis=0, tiled=True)  7.23 us
    reshape x1, local copies, waits for them, and re-layouts, shards(): part_a.reshape(1 * lax.axis_size('blk'), rows_a * rank)  5.61 us
  transfers between devices with their start and end apart: 3, of which 3 were waited for; matrix products, arithmetic and copies ran while one was open for 6% of the time, Pallas kernels for 0%

commit v1 on v0

v1 whole, which is shorter than its diff:
```python
import functools
import math

import jax
import jax.numpy as jnp
from jax import lax
from jax.experimental import pallas as pl
from jax.experimental.pallas import tpu as pltpu
from jax.sharding import PartitionSpec as P

MESH = pl.DeviceIdType.MESH
BF16, F32 = jnp.bfloat16, jnp.float32


def dot(left, right, contract):
    return lax.dot_general(left, right, (contract, ((), ())), preferred_element_type=F32)


def kernel(sizes, tok_hbm, gk_hbm, a_ref, b_ref, oa_ref, ob_ref, *scratch):
    nz, ny, nd, pad, factor = sizes
    nblk = nz * ny
    tok, gk, spread, pb, load_sem = scratch[:5]
    half = (len(scratch) - 5) // 2
    names = ["g", "gzs", "gzr", "gys", "gyr", "gcs", "gcr", "pp", "sc", "rc", "rcs", "rcr"]
    names += ["sy", "ry", "rys", "ryr", "sz", "rz", "rzs", "rzr", "rx", "rxs", "rxr", "fin", "fs", "fr"]
    fam_a = dict(zip(names, scratch[5 : 5 + half]))
    fam_b = dict(zip(names, scratch[5 + half :]))
    rows_b = b_ref.shape[0]
    blk, dp = lax.axis_index("blk"), lax.axis_index("dp")
    z, y = lax.div(blk, ny), lax.rem(blk, ny)
    d, c = lax.div(dp, 2), lax.rem(dp, 2)
    peer = (blk, d * 2 + (1 - c))

    def near(zo, yo):
        return lax.rem(z + zo + nz, nz) * ny + lax.rem(y + yo + ny, ny)

    def away(xo):
        return lax.rem(d + xo + nd, nd)

    load_tok = pltpu.make_async_copy(tok_hbm, tok, load_sem.at[0])
    load_gk = pltpu.make_async_copy(gk_hbm, gk, load_sem.at[1])
    load_gk.start()
    load_tok.start()

    barrier = pltpu.get_barrier_semaphore()
    others = [(near(zo, 0), dp) for zo in range(1, nz)]
    others += [(near(0, yo), dp) for yo in range(1, ny)]
    others += [(blk, away(xo) * 2 + c) for xo in range(1, nd)] + [peer]
    for other in others:
        pl.semaphore_signal(barrier, inc=1, device_id=other, device_id_type=MESH)

    wide = fam_b["g"].shape[3]
    fam_b["g"][blk] = jnp.zeros(fam_b["g"].shape[1:], BF16)
    fam_b["g"][blk, 0, :rows_b] = b_ref[:, :wide]
    fam_b["g"][blk, 1, :rows_b] = b_ref[:, wide:]
    fam_a["g"][blk] = a_ref[...].T.reshape(fam_a["g"].shape[1:])
    pl.semaphore_wait(barrier, len(others))

    sent = []

    def rcopy(src, dst, ssem, rsem, device):
        return pltpu.make_async_remote_copy(
            src_ref=src, dst_ref=dst, send_sem=ssem, recv_sem=rsem,
            device_id=device, device_id_type=MESH,
        )

    def send(*args):
        copy = rcopy(*args)
        copy.start()
        sent.append(copy)

    def g_z(f, zo, at):
        part = f["g"].at[at, c]
        return part, part, f["gzs"].at[zo - 1], f["gzr"].at[zo - 1], (near(zo, 0), dp)

    def g_y(f, zo, yo, at):
        part = f["g"].at[at, c]
        return part, part, f["gys"].at[yo - 1, zo], f["gyr"].at[yo - 1, zo], (near(0, yo), dp)

    def g_c(f, zo, yo, at, side):
        k = yo * nz + zo - 1
        part = f["g"].at[at, side]
        return part, part, f["gcs"].at[k], f["gcr"].at[k], peer

    def gather_start(f):
        for zo in range(1, nz):
            send(*g_z(f, zo, blk))
        for yo in range(1, ny):
            send(*g_y(f, 0, yo, blk))

    def gather_z(f):
        for zo in range(1, nz):
            at = near(-zo, 0)
            rcopy(*g_z(f, zo, at)).wait_recv()
            for yo in range(1, ny):
                send(*g_y(f, zo, yo, at))
            send(*g_c(f, zo, 0, at, c))

    def gather_y(f):
        for zo in range(nz):
            for yo in range(1, ny):
                at = near(-zo, -yo)
                rcopy(*g_y(f, zo, yo, at)).wait_recv()
                send(*g_c(f, zo, yo, at, c))

    def gathered(f, zo, yo):
        at = near(-zo, -yo)
        if zo or yo:
            rcopy(*g_c(f, zo, yo, at, 1 - c)).wait_recv()
        return at

    def r_c(f, zo, yo):
        k = yo * nz + zo
        return f["sc"].at[k], f["rc"].at[k], f["rcs"].at[k], f["rcr"].at[k], peer

    def r_y(f, zo, yo):
        i = (yo - 1, zo)
        return f["sy"].at[i], f["ry"].at[i], f["rys"].at[i], f["ryr"].at[i], (near(0, yo), dp)

    def r_z(f, zo):
        i = zo - 1
        return f["sz"].at[i], f["rz"].at[i], f["rzs"].at[i], f["rzr"].at[i], (near(zo, 0), dp)

    def r_x(f, xo, at):
        part = f["rx"].at[at]
        return part, part, f["rxs"].at[xo - 1], f["rxr"].at[xo - 1], (blk, away(xo) * 2 + c)

    def r_f(f, side):
        part = f["fin"].at[side]
        return part, part, f["fs"], f["fr"], peer

    order = list(range(1, nz)) + [0]

    def reduce_start(f, zo, yo, mine, theirs):
        k = yo * nz + zo
        f["sc"][k] = theirs.astype(BF16)
        send(*r_c(f, zo, yo))
        f["pp"][k] = mine

    def chip_sum(f, zo, yo):
        k = yo * nz + zo
        rcopy(*r_c(f, zo, yo)).wait_recv()
        return f["pp"][k] + f["rc"][k].astype(F32)

    def reduce_y(f):
        for zo in order:
            for yo in range(1, ny):
                f["sy"][yo - 1, zo] = chip_sum(f, zo, yo).astype(BF16)
                send(*r_y(f, zo, yo))

    def reduce_z(f):
        for zo in order:
            total = chip_sum(f, zo, 0)
            for yo in range(1, ny):
                rcopy(*r_y(f, zo, yo)).wait_recv()
                total = total + f["ry"][yo - 1, zo].astype(F32)
            if zo:
                f["sz"][zo - 1] = total.astype(BF16)
                send(*r_z(f, zo))
            else:
                f["pp"][0] = total

    def reduce_x(f):
        total = f["pp"][0]
        for zo in range(1, nz):
            rcopy(*r_z(f, zo)).wait_recv()
            total = total + f["rz"][zo - 1].astype(F32)
        f["rx"][d] = total * factor
        for xo in range(1, nd):
            send(*r_x(f, xo, d))

    def reduce_last(f):
        for xo in range(1, nd):
            rcopy(*r_x(f, xo, away(-xo))).wait_recv()
        total = f["rx"][0]
        for at in range(1, nd):
            total = total + f["rx"][at]
        f["fin"][c] = total
        send(*r_f(f, c))

    def finish(f, out):
        rcopy(*r_f(f, 1 - c)).wait_recv()
        out[...] = f["fin"][...]

    gather_start(fam_b)
    gather_start(fam_a)
    gather_z(fam_b)
    gather_y(fam_b)

    rank = a_ref.shape[1]
    shape = (rank, nblk * pad)
    row, col = lax.broadcasted_iota(jnp.int32, shape, 0), lax.broadcasted_iota(jnp.int32, shape, 1)
    place = lax.rem(col, pad)
    pick = (row == lax.div(col, pad) * rows_b + place) & (place < rows_b)
    pick = jnp.where(pick, 1.0, 0.0).astype(BF16)
    gather_z(fam_a)
    for yo in range(ny):
        for zo in range(nz):
            gathered(fam_b, zo, yo)
    load_gk.wait()
    flow = jnp.zeros((rank, tok.shape[0]), F32)
    for s in range(2):
        factor_b = dot(pick, fam_b["g"][:, s].reshape(nblk * pad, wide), ((1,), (0,))).astype(BF16)
        flow = flow + dot(factor_b, gk[:, s * wide : (s + 1) * wide], ((1,), (1,)))
    spread[...] = flow.astype(BF16).reshape(spread.shape)
    both = jnp.concatenate([spread[c], spread[1 - c]], axis=0)

    cols = fam_a["g"].shape[3]

    def tok_part(at):
        return tok[:, pl.ds(pl.multiple_of(at * cols, cols), cols)]

    load_tok.wait()
    for yo in list(range(1, ny)) + [0]:
        for zo in order:
            part = dot(both, tok_part(near(zo, yo)), ((1,), (0,)))
            reduce_start(fam_a, zo, yo, part[: rank // 2], part[rank // 2 :])
    gather_y(fam_a)
    reduce_y(fam_a)
    hidden = jnp.zeros((rank, tok.shape[0]), F32)
    for yo in range(ny):
        for zo in range(nz):
            at = gathered(fam_a, zo, yo)
            hidden = hidden + dot(fam_a["g"][at].reshape(rank, cols), tok_part(at), ((1,), (1,)))
    hidden = dot(pick, hidden.astype(BF16), ((0,), (0,))).astype(BF16)
    pb[...] = dot(hidden, gk[...], ((1,), (0,)))
    for yo in list(range(1, ny)) + [0]:
        for zo in order:
            lines = pl.ds(pl.multiple_of(near(zo, yo) * pad, pad), pad)
            mine = pb[lines, pl.ds(pl.multiple_of(c * wide, wide), wide)]
            theirs = pb[lines, pl.ds(pl.multiple_of((1 - c) * wide, wide), wide)]
            reduce_start(fam_b, zo, yo, mine, theirs)
    reduce_z(fam_a)
    reduce_y(fam_b)
    reduce_z(fam_b)
    reduce_x(fam_a)
    reduce_x(fam_b)
    reduce_last(fam_a)
    reduce_last(fam_b)
    finish(fam_a, oa_ref)
    finish(fam_b, ob_ref)
    for copy in sent:
        copy.wait_send()


def family(nz, ny, nd, h, w):
    vm, dma = pltpu.VMEM, pltpu.SemaphoreType.DMA
    n = nz * ny
    return [
        vm((n, 2, h, w), BF16), dma((nz - 1,)), dma((nz - 1,)),
        dma((ny - 1, nz)), dma((ny - 1, nz)), dma((n - 1,)), dma((n - 1,)),
        vm((n, h, w), F32), vm((n, h, w), BF16), vm((n, h, w), BF16), dma((n,)), dma((n,)),
        vm((ny - 1, nz, h, w), BF16), vm((ny - 1, nz, h, w), BF16),
        dma((ny - 1, nz)), dma((ny - 1, nz)),
        vm((nz - 1, h, w), BF16), vm((nz - 1, h, w), BF16), dma((nz - 1,)), dma((nz - 1,)),
        vm((nd, h, w), F32), dma((nd - 1,)), dma((nd - 1,)),
        vm((2, h, w), F32), dma(()), dma(()),
    ]


def shards(tokens, grad_k, adapter_a, adapter_b):
    nblk, ndp = lax.axis_size("blk"), lax.axis_size("dp")
    ny = 2 ** (int(math.log2(nblk)) // 2)
    nz, nd = nblk // ny, ndp // 2
    rows_a, rank = adapter_a.shape
    rows_b, width = adapter_b.shape
    pad = -(-rows_b // 16) * 16
    count = tokens.shape[0]
    factor = 1.0 / math.sqrt(count * nblk * ndp)
    sizes_a, sizes_b = (rank // 2, rows_a), (pad, width // 2)
    vmem, anywhere = pl.BlockSpec(memory_space=pltpu.VMEM), pl.BlockSpec(memory_space=pl.ANY)
    out_a, out_b = pl.pallas_call(
        functools.partial(kernel, (nz, ny, nd, pad, factor)),
        out_shape=[jax.ShapeDtypeStruct((2, *s), F32) for s in (sizes_a, sizes_b)],
        in_specs=[anywhere, anywhere, vmem, vmem],
        out_specs=[vmem, vmem],
        scratch_shapes=[
            pltpu.VMEM(tokens.shape, BF16),
            pltpu.VMEM(grad_k.shape, BF16),
            pltpu.VMEM((2, rank // 2, count), BF16),
            pltpu.VMEM((nblk * pad, width), F32),
            pltpu.SemaphoreType.DMA((2,)),
            *family(nz, ny, nd, *sizes_a),
            *family(nz, ny, nd, *sizes_b),
        ],
        compiler_params=pltpu.CompilerParams(
            collective_id=0, has_side_effects=True, vmem_limit_bytes=52 * 2**20
        ),
        cost_estimate=pl.CostEstimate(
            flops=4 * count * rank * (tokens.shape[1] + width),
            bytes_accessed=2 * count * (tokens.shape[1] + width),
            transcendentals=0,
        ),
    )(tokens, grad_k, adapter_a, adapter_b)
    grad_a = out_a.reshape(rank, rows_a).T
    grad_b = jnp.concatenate([out_b[0, :rows_b], out_b[1, :rows_b]], axis=1)
    return grad_a, grad_b


def solution(mesh):
    return jax.shard_map(
        shards,
        mesh=mesh,
        in_specs=(P(("blk", "dp"), None), P(("blk", "dp"), None), P("blk", None), P("blk", None)),
        out_specs=(P("blk", None), P("blk", None)),
        check_vma=False,
    )
```

time: 269 us -> 50.3 us (0.19)
  waiting for transfers between devices: 187 us -> 0 us
  Pallas kernels: 0 us -> 45.1 us
  blocking collectives: 27.2 us -> 0 us
  local copies, waits for them, and re-layouts: 24.9 us -> 3.74 us
  between operations: 13.8 us -> 0.66 us
  matrix products: 8.45 us -> 0 us
  other arithmetic: 4.34 us -> 0.65 us
    unnamed x4 -> x0, waiting for transfers between devices: 148 us -> none
    pallas_call x0 -> x1, Pallas kernels: none -> 45.1 us  [shards(): pl.pallas_call(functools.partial(kernel, (nz, ny, nd, pad, factor)), out_...]
    psum x1 -> x0, waiting for transfers between devices: 31.9 us -> none  [shards(): grad_a, grad_b = lax.psum((owned_a, owned_b), 'dp')]
    all_gather x1 -> x0, blocking collectives: 27.2 us -> none  [shards(): lax.all_gather(adapter_b, 'blk', axis=0, tiled=True)]
    dot_general x2 -> x0, matrix products: 8.45 us -> none  [the longest x1 4.23 us: shards(): lax.dot_general(columns, spread, (((0,), (0,)), ((), ())), preferred_elem...]
    reshape x2 -> x0, local copies, waits for them, and re-layouts: 7.76 us -> none  [the longest x1 5.61 us: shards(): part_a.reshape(1 * lax.axis_size('blk'), rows_a * rank)]
    all_gather x1 -> x0, waiting for transfers between devices: 7.23 us -> none  [shards(): lax.all_gather(adapter_a, 'blk', axis=0, tiled=True)]
    slice x2 -> x0, local copies, waits for them, and re-layouts: 5.68 us -> none  [the longest x1 3.58 us: shards(): owned_a = share[0, :rows_a * rank].reshape(rows_a, rank)]
  transfers between devices with their start and end apart: 3 -> 0, of which waited for: 3 -> 0; matrix products, arithmetic and copies ran while one was open for 6% -> 0% of each run, Pallas kernels for 0% -> 0%
where the time goes in v1:
time: 50.3 us; the launch traced here: 50.1 us
  Pallas kernels  45.1 us (90%)
  local copies, waits for them, and re-layouts  3.74 us (7%)
  between operations  0.66 us (1%)
  other arithmetic  0.65 us (1%)
    pallas_call x1, Pallas kernels, shards(): pl.pallas_call(functools.partial(kernel, (nz, ny, nd, pad, factor)), out_...  45.1 us
    unnamed x6, local copies, waits for them, and re-layouts  3.73 us

profile of v1, /device:TPU:1, one launch (start us, length us, event | category | flops | bytes accessed | tf_op | source)
XLA Modules:
  0.0 50.1 jit_solution(17160527441369781822)
XLA Ops:
  0.6 1.1 %copy.6.a_ref = bf16[512,192]{1,0:T(8,128)(2,1)S(1)} copy(bf16[512,192]{0,1:T(8,128)(2,1)} %param.6) | data formatting | bytes 393216 | tf_op args[2]
  1.7 0.0 copy-start
  1.7 1.1 %copy-done = bf16[384,1024]{1,0:T(8,128)(2,1)S(1)} copy-done((bf16[384,1024]{1,0:T(8,128)(2,1)S(1)}, bf16[384,1024]{1,0:T(8,128)(2,1)}, u32[]{:S(2)}) %copy-start) | copy-done | bytes 786456
  2.8 0.0 copy-start.1
  2.8 0.8 %copy-done.1 = bf16[24,1024]{1,0:T(8,128)(2,1)S(1)} copy-done((bf16[24,1024]{1,0:T(8,128)(2,1)S(1)}, bf16[24,1024]{1,0:T(8,128)(2,1)}, u32[]{:S(2)}) %copy-start.1) | copy-done | bytes 49176
  3.6 45.1 %shard_map.59 = (f32[2,96,512]{2,1,0:T(8,128)S(1)}, f32[2,32,512]{2,1,0:T(8,128)S(1)}) custom-call(bf16[384,4096]{1,0:T(8,128)(2,1)} %tok_hbm.1, bf16[384,1024]{1,0:T(8,128)(2,1)S(1)} %copy-done, bf16[512,192]{1,0:T(8,128)(2,1)S(1)} %copy.6.a_ref, bf16[24,1024]{1,0:T(8,128)(2,1)S(1)} %copy-done.1), custom_call_target="tpu_custom_call" | custom-call | flops 1509949440 | bytes 3932160 | tf_op jit(solution)/shard_map/pallas_call | solution.py:272
  48.7 0.6 %pad_maximum_fusion = f32[24,1024]{1,0:T(8,128)} fusion(f32[24,512]{1,0:T(8,128)S(1)} %get-tuple-element.7, f32[24,512]{1,0:T(8,128)S(1)} %get-tuple-element.6), kind=kLoop, calls=%fused_computation | loop fusion | flops 24576 | bytes 196608 | tf_op jit(solution)/shard_map/concatenate | solution.py:296
  49.4 0.7 %copy.8 = f32[512,192]{0,1:T(8,128)} copy(f32[512,192]{0,1:T(8,128)S(1)} %bitcast.7) | data formatting | bytes 786432
  (1 shorter events, 0.0 us)
Async XLA Ops:
  1.7 1.1 %copy-start = (bf16[384,1024]{1,0:T(8,128)(2,1)S(1)}, bf16[384,1024]{1,0:T(8,128)(2,1)}, u32[]{:S(2)}) copy-start(bf16[384,1024]{1,0:T(8,128)(2,1)} %gk_hbm.1) | copy-start | bytes 2359300
  2.8 0.8 %copy-start.1 = (bf16[24,1024]{1,0:T(8,128)(2,1)S(1)}, bf16[24,1024]{1,0:T(8,128)(2,1)}, u32[]{:S(2)}) copy-start(bf16[24,1024]{1,0:T(8,128)(2,1)} %b_ref.1) | copy-start | bytes 147460

commit v2 on v1

--- a/solution.py
+++ b/solution.py
@@ -10,26 +10,30 @@
 
 MESH = pl.DeviceIdType.MESH
 BF16, F32 = jnp.bfloat16, jnp.float32
+HP = 48
 
 
 def dot(left, right, contract):
     return lax.dot_general(left, right, (contract, ((), ())), preferred_element_type=F32)
 
 
-def kernel(sizes, tok_hbm, gk_hbm, a_ref, b_ref, oa_ref, ob_ref, *scratch):
-    nz, ny, nd, pad, factor = sizes
+def kernel(sizes, tok_hbm, gk_hbm, a_hbm, b_hbm, oa_ref, ob_ref, *scratch):
+    nz, ny, nd, pad, hp, factor = sizes
     nblk = nz * ny
-    tok, gk, spread, pb, load_sem = scratch[:5]
-    half = (len(scratch) - 5) // 2
+    tok, gk, own_b, spread, pb, load_sem = scratch[:6]
+    half = 26
     names = ["g", "gzs", "gzr", "gys", "gyr", "gcs", "gcr", "pp", "sc", "rc", "rcs", "rcr"]
     names += ["sy", "ry", "rys", "ryr", "sz", "rz", "rzs", "rzr", "rx", "rxs", "rxr", "fin", "fs", "fr"]
-    fam_a = dict(zip(names, scratch[5 : 5 + half]))
-    fam_b = dict(zip(names, scratch[5 + half :]))
-    rows_b = b_ref.shape[0]
+    fam_a = dict(zip(names, scratch[6 : 6 + half]))
+    fam_b = dict(zip(names, scratch[6 + half : 6 + 2 * half]))
+    names_q = ["sx", "rx", "sxs", "rxr", "sy", "ry", "rys", "ryr", "sz", "rz", "rzs", "rzr"]
+    fam_q = dict(zip(names_q + ["fin", "fs", "fr"], scratch[6 + 2 * half :]))
+    rows_b = b_hbm.shape[0]
     blk, dp = lax.axis_index("blk"), lax.axis_index("dp")
     z, y = lax.div(blk, ny), lax.rem(blk, ny)
     d, c = lax.div(dp, 2), lax.rem(dp, 2)
     peer = (blk, d * 2 + (1 - c))
+    across = (blk, (1 - d) * 2 + c)
 
     def near(zo, yo):
         return lax.rem(z + zo + nz, nz) * ny + lax.rem(y + yo + ny, ny)
@@ -39,8 +43,10 @@
 
     load_tok = pltpu.make_async_copy(tok_hbm, tok, load_sem.at[0])
     load_gk = pltpu.make_async_copy(gk_hbm, gk, load_sem.at[1])
-    load_gk.start()
-    load_tok.start()
+    load_a = pltpu.make_async_copy(a_hbm, fam_a["g"].at[blk], load_sem.at[2])
+    load_b = pltpu.make_async_copy(b_hbm, own_b, load_sem.at[3])
+    for load in (load_b, load_a, load_gk, load_tok):
+        load.start()
 
     barrier = pltpu.get_barrier_semaphore()
     others = [(near(zo, 0), dp) for zo in range(1, nz)]
@@ -51,9 +57,10 @@
 
     wide = fam_b["g"].shape[3]
     fam_b["g"][blk] = jnp.zeros(fam_b["g"].shape[1:], BF16)
-    fam_b["g"][blk, 0, :rows_b] = b_ref[:, :wide]
-    fam_b["g"][blk, 1, :rows_b] = b_ref[:, wide:]
-    fam_a["g"][blk] = a_ref[...].T.reshape(fam_a["g"].shape[1:])
+    load_b.wait()
+    fam_b["g"][blk, 0, :rows_b] = own_b[:, :wide]
+    fam_b["g"][blk, 1, :rows_b] = own_b[:, wide:]
+    load_a.wait()
     pl.semaphore_wait(barrier, len(others))
 
     sent = []
@@ -159,6 +166,47 @@
                 send(*r_z(f, zo))
             else:
                 f["pp"][0] = total
+
+    def q_x(k):
+        return fam_q["sx"].at[k], fam_q["rx"].at[k], fam_q["sxs"].at[k], fam_q["rxr"].at[k], across
+
+    def q_last(at):
+        part = fam_q["fin"].at[at]
+        return part, part, fam_q["fs"], fam_q["fr"], across
+
+    def cols_of(at):
+        narrow = fam_a["pp"].shape[2] // 2
+        return pl.ds(pl.multiple_of(at * narrow, narrow), narrow)
+
+    def spread_out(f, zo, yo):
+        k = yo * nz + zo
+        f["pp"][k] = chip_sum(f, zo, yo)
+        if fam_q:
+            fam_q["sx"][k] = f["pp"][k, hp:, cols_of(1 - d)].astype(BF16)
+            send(*q_x(k))
+        if yo:
+            f["sy"][yo - 1, zo] = f["pp"][k, :hp].astype(BF16)
+            send(*r_y(f, zo, yo))
+
+    def q_sum(zo, yo):
+        k = yo * nz + zo
+        rcopy(*q_x(k)).wait_recv()
+        return fam_a["pp"][k, hp:, cols_of(d)] + fam_q["rx"][k].astype(F32)
+
+    def y_sum(f, zo, total):
+        for yo in range(1, ny):
+            rcopy(*r_y(f, zo, yo)).wait_recv()
+            total = total + f["ry"][yo - 1, zo].astype(F32)
+        if zo:
+            f["sz"][zo - 1] = total.astype(BF16)
+            send(*r_z(f, zo))
+        return total
+
+    def z_sum(f, total):
+        for zo in range(1, nz):
+            rcopy(*r_z(f, zo)).wait_recv()
+            total = total + f["rz"][zo - 1].astype(F32)
+        return total * factor
 
     def reduce_x(f):
         total = f["pp"][0]
@@ -187,7 +235,7 @@
     gather_z(fam_b)
     gather_y(fam_b)
 
-    rank = a_ref.shape[1]
+    rank = 2 * a_hbm.shape[1]
     shape = (rank, nblk * pad)
     row, col = lax.broadcasted_iota(jnp.int32, shape, 0), lax.broadcasted_iota(jnp.int32, shape, 1)
     place = lax.rem(col, pad)
@@ -216,7 +264,14 @@
             part = dot(both, tok_part(near(zo, yo)), ((1,), (0,)))
             reduce_start(fam_a, zo, yo, part[: rank // 2], part[rank // 2 :])
     gather_y(fam_a)
-    reduce_y(fam_a)
+    for yo in [*range(1, ny), 0]:
+        for zo in order:
+            spread_out(fam_a, zo, yo)
+    if fam_q:
+        for zo in order:
+            for yo in range(1, ny):
+                fam_q["sy"][yo - 1, zo] = q_sum(zo, yo).astype(BF16)
+                send(*r_y(fam_q, zo, yo))
     hidden = jnp.zeros((rank, tok.shape[0]), F32)
     for yo in range(ny):
         for zo in range(nz):
@@ -230,12 +285,32 @@
             mine = pb[lines, pl.ds(pl.multiple_of(c * wide, wide), wide)]
             theirs = pb[lines, pl.ds(pl.multiple_of((1 - c) * wide, wide), wide)]
             reduce_start(fam_b, zo, yo, mine, theirs)
-    reduce_z(fam_a)
+    for zo in order:
+        own = y_sum(fam_a, zo, fam_a["pp"][zo, :hp])
+    if fam_q:
+        for zo in order:
+            own_q = y_sum(fam_q, zo, q_sum(zo, 0))
     reduce_y(fam_b)
     reduce_z(fam_b)
-    reduce_x(fam_a)
+    fam_a["rx"][d] = z_sum(fam_a, own)
+    for xo in range(1, nd):
+        send(*r_x(fam_a, xo, d))
+    if fam_q:
+        fam_q["fin"][d] = z_sum(fam_q, own_q)
+        send(*q_last(d))
     reduce_x(fam_b)
-    reduce_last(fam_a)
+    for xo in range(1, nd):
+        rcopy(*r_x(fam_a, xo, away(-xo))).wait_recv()
+    total = fam_a["rx"][0]
+    for at in range(1, nd):
+        total = total + fam_a["rx"][at]
+    fam_a["fin"][c, :hp] = total
+    if fam_q:
+        rcopy(*q_last(1 - d)).wait_recv()
+        narrow = cols // 2
+        fam_a["fin"][c, hp:, :narrow] = fam_q["fin"][0]
+        fam_a["fin"][c, hp:, narrow:] = fam_q["fin"][1]
+    send(*r_f(fam_a, c))
     reduce_last(fam_b)
     finish(fam_a, oa_ref)
     finish(fam_b, ob_ref)
@@ -243,17 +318,29 @@
         copy.wait_send()
 
 
-def family(nz, ny, nd, h, w):
+def family(nz, ny, nd, h, w, hp):
     vm, dma = pltpu.VMEM, pltpu.SemaphoreType.DMA
     n = nz * ny
     return [
         vm((n, 2, h, w), BF16), dma((nz - 1,)), dma((nz - 1,)),
         dma((ny - 1, nz)), dma((ny - 1, nz)), dma((n - 1,)), dma((n - 1,)),
         vm((n, h, w), F32), vm((n, h, w), BF16), vm((n, h, w), BF16), dma((n,)), dma((n,)),
+        vm((ny - 1, nz, hp, w), BF16), vm((ny - 1, nz, hp, w), BF16),
+        dma((ny - 1, nz)), dma((ny - 1, nz)),
+        vm((nz - 1, hp, w), BF16), vm((nz - 1, hp, w), BF16), dma((nz - 1,)), dma((nz - 1,)),
+        vm((nd, hp, w), F32), dma((nd - 1,)), dma((nd - 1,)),
+        vm((2, h, w), F32), dma(()), dma(()),
+    ]
+
+
+def family_q(nz, ny, h, w):
+    vm, dma = pltpu.VMEM, pltpu.SemaphoreType.DMA
+    n = nz * ny
+    return [
+        vm((n, h, w), BF16), vm((n, h, w), BF16), dma((n,)), dma((n,)),
         vm((ny - 1, nz, h, w), BF16), vm((ny - 1, nz, h, w), BF16),
         dma((ny - 1, nz)), dma((ny - 1, nz)),
         vm((nz - 1, h, w), BF16), vm((nz - 1, h, w), BF16), dma((nz - 1,)), dma((nz - 1,)),
-        vm((nd, h, w), F32), dma((nd - 1,)), dma((nd - 1,)),
         vm((2, h, w), F32), dma(()), dma(()),
     ]
 
@@ -268,30 +355,35 @@
     count = tokens.shape[0]
     factor = 1.0 / math.sqrt(count * nblk * ndp)
     sizes_a, sizes_b = (rank // 2, rows_a), (pad, width // 2)
+    two = nd == 2 and rank % 64 == 0 and rows_a % 256 == 0
+    hp = HP if two else rank // 2
+    second = family_q(nz, ny, rank // 2 - hp, rows_a // 2) if two else []
     vmem, anywhere = pl.BlockSpec(memory_space=pltpu.VMEM), pl.BlockSpec(memory_space=pl.ANY)
     out_a, out_b = pl.pallas_call(
-        functools.partial(kernel, (nz, ny, nd, pad, factor)),
+        functools.partial(kernel, (nz, ny, nd, pad, hp, factor)),
         out_shape=[jax.ShapeDtypeStruct((2, *s), F32) for s in (sizes_a, sizes_b)],
-        in_specs=[anywhere, anywhere, vmem, vmem],
+        in_specs=[anywhere] * 4,
         out_specs=[vmem, vmem],
         scratch_shapes=[
             pltpu.VMEM(tokens.shape, BF16),
             pltpu.VMEM(grad_k.shape, BF16),
+            pltpu.VMEM(adapter_b.shape, BF16),
             pltpu.VMEM((2, rank // 2, count), BF16),
             pltpu.VMEM((nblk * pad, width), F32),
-            pltpu.SemaphoreType.DMA((2,)),
-            *family(nz, ny, nd, *sizes_a),
-            *family(nz, ny, nd, *sizes_b),
+            pltpu.SemaphoreType.DMA((4,)),
+            *family(nz, ny, nd, *sizes_a, hp),
+            *family(nz, ny, nd, *sizes_b, pad),
+            *second,
         ],
         compiler_params=pltpu.CompilerParams(
-            collective_id=0, has_side_effects=True, vmem_limit_bytes=52 * 2**20
+            collective_id=0, has_side_effects=True, vmem_limit_bytes=62 * 2**20
         ),
         cost_estimate=pl.CostEstimate(
             flops=4 * count * rank * (tokens.shape[1] + width),
             bytes_accessed=2 * count * (tokens.shape[1] + width),
             transcendentals=0,
         ),
-    )(tokens, grad_k, adapter_a, adapter_b)
+    )(tokens, grad_k, adapter_a.T.reshape(2, rank // 2, rows_a), adapter_b)
     grad_a = out_a.reshape(rank, rows_a).T
     grad_b = jnp.concatenate([out_b[0, :rows_b], out_b[1, :rows_b]], axis=1)
     return grad_a, grad_b

time: 50.3 us -> 48.8 us (0.970)
  local copies, waits for them, and re-layouts: 3.74 us -> 2.6 us
    unnamed x6 -> x1, local copies, waits for them, and re-layouts: 3.73 us -> 1.77 us
    squeeze x1, local copies, waits for them, and re-layouts: 0.01 us -> 0.83 us  [shards(): grad_b = jnp.concatenate([out_b[0, :rows_b], out_b[1, :rows_b]], axis=1)]
where the time goes in v2:
time: 48.8 us; the launch traced here: 48.6 us
  Pallas kernels  44.7 us (92%)
  local copies, waits for them, and re-layouts  2.6 us (5%)
  other arithmetic  0.65 us (1%)
  between operations  0.64 us (1%)
    pallas_call x1, Pallas kernels, shards(): pl.pallas_call(functools.partial(kernel, (nz, ny, nd, pad, hp, factor)),...  44.7 us
    unnamed x1, local copies, waits for them, and re-layouts  1.77 us

profile of v2, /device:TPU:1, one launch (start us, length us, event | category | flops | bytes accessed | tf_op | source)
XLA Modules:
  0.0 48.6 jit_solution(8018296585688491887)
XLA Ops:
  0.6 44.7 %shard_map.59 = (f32[2,96,512]{2,1,0:T(8,128)}, f32[2,32,512]{2,1,0:T(8,128)}) custom-call(bf16[384,4096]{1,0:T(8,128)(2,1)} %tok_hbm.1, bf16[384,1024]{1,0:T(8,128)(2,1)} %gk_hbm.1, bf16[2,96,512]{2,1,0:T(8,128)(2,1)} %bitcast.11, bf16[24,1024]{1,0:T(8,128)(2,1)} %b_hbm.1), custom_call_target="tpu_custom_call" | custom-call | flops 1509949440 | bytes 3932160 | tf_op jit(solution)/shard_map/pallas_call | solution.py:362
  45.4 0.8 %slice_bitcast_fusion.1 = (f32[24,512]{1,0:T(8,128)S(1)}, f32[24,512]{1,0:T(8,128)S(1)}) fusion(f32[2,32,512]{2,1,0:T(8,128)} %get-tuple-element.5), kind=kLoop, calls=%fused_computation.2 | loop fusion | bytes 196608 | tf_op jit(solution)/shard_map/squeeze | solution.py:388
  46.2 0.6 %pad_maximum_fusion = f32[24,1024]{1,0:T(8,128)} fusion(f32[24,512]{1,0:T(8,128)S(1)} %get-tuple-element.7, f32[24,512]{1,0:T(8,128)S(1)} %get-tuple-element.6), kind=kLoop, calls=%fused_computation | loop fusion | flops 24576 | bytes 196608 | tf_op jit(solution)/shard_map/concatenate | solution.py:388
  46.8 1.8 %copy.7 = f32[512,192]{0,1:T(8,128)} copy(f32[512,192]{0,1:T(8,128)} %bitcast.10) | data formatting | bytes 786432

commit v3 on v2

--- a/solution.py
+++ b/solution.py
@@ -263,10 +263,10 @@
         for zo in order:
             part = dot(both, tok_part(near(zo, yo)), ((1,), (0,)))
             reduce_start(fam_a, zo, yo, part[: rank // 2], part[rank // 2 :])
+    for yo in [*range(1, ny), 0]:
+        for zo in order:
+            spread_out(fam_a, zo, yo)
     gather_y(fam_a)
-    for yo in [*range(1, ny), 0]:
-        for zo in order:
-            spread_out(fam_a, zo, yo)
     if fam_q:
         for zo in order:
             for yo in range(1, ny):

time: 48.8 us -> 48 us (0.984)
  Pallas kernels: 44.7 us -> 43.9 us
    pallas_call x1, Pallas kernels: 44.7 us -> 43.9 us  [shards(): pl.pallas_call(functools.partial(kernel, (nz, ny, nd, pad, hp, factor)),...]
where the time goes in v3:
time: 48 us; the launch traced here: 47.8 us
  Pallas kernels  43.9 us (91%)
  local copies, waits for them, and re-layouts  2.6 us (5%)
  other arithmetic  0.65 us (1%)
  between operations  0.64 us (1%)
    pallas_call x1, Pallas kernels, shards(): pl.pallas_call(functools.partial(kernel, (nz, ny, nd, pad, hp, factor)),...  43.9 us
    unnamed x1, local copies, waits for them, and re-layouts  1.77 us

profile of v3, /device:TPU:1, one launch (start us, length us, event | category | flops | bytes accessed | tf_op | source)
XLA Modules:
  0.0 47.8 jit_solution(6445494567346972100)
XLA Ops:
  0.6 43.9 %shard_map.59 = (f32[2,96,512]{2,1,0:T(8,128)}, f32[2,32,512]{2,1,0:T(8,128)}) custom-call(bf16[384,4096]{1,0:T(8,128)(2,1)} %tok_hbm.1, bf16[384,1024]{1,0:T(8,128)(2,1)} %gk_hbm.1, bf16[2,96,512]{2,1,0:T(8,128)(2,1)} %bitcast.11, bf16[24,1024]{1,0:T(8,128)(2,1)} %b_hbm.1), custom_call_target="tpu_custom_call" | custom-call | flops 1509949440 | bytes 3932160 | tf_op jit(solution)/shard_map/pallas_call | solution.py:362
  44.5 0.8 %slice_bitcast_fusion.1 = (f32[24,512]{1,0:T(8,128)S(1)}, f32[24,512]{1,0:T(8,128)S(1)}) fusion(f32[2,32,512]{2,1,0:T(8,128)} %get-tuple-element.5), kind=kLoop, calls=%fused_computation.2 | loop fusion | bytes 196608 | tf_op jit(solution)/shard_map/squeeze | solution.py:388
  45.4 0.6 %pad_maximum_fusion = f32[24,1024]{1,0:T(8,128)} fusion(f32[24,512]{1,0:T(8,128)S(1)} %get-tuple-element.7, f32[24,512]{1,0:T(8,128)S(1)} %get-tuple-element.6), kind=kLoop, calls=%fused_computation | loop fusion | flops 24576 | bytes 196608 | tf_op jit(solution)/shard_map/concatenate | solution.py:388
  46.0 1.8 %copy.7 = f32[512,192]{0,1:T(8,128)} copy(f32[512,192]{0,1:T(8,128)} %bitcast.10) | data formatting | bytes 786432
